TPU v7x, 32 devices: a whole 2x2x4 slice. The times are simulated.
32 devices in a mesh: row: 4 (over z), ma: 8 (over y, x, core).
Axes of the slice: x: 2, y: 2, z: 4, core: 2. Of those that a mesh axis runs over, the one named last changes fastest.
Arguments:
- spectra: float32 [4, 2, 128, 4224], P(None, None, 'row', 'ma'), may hold values from -6 to 6
- dtheta_table: bfloat16 [4224, 768], P('ma'), may hold values from -0.046875 to 0.046875
- dphi_table: bfloat16 [4224, 768], P('ma'), may hold values from -0.046875 to 0.046875
- analysis_table: bfloat16 [4224, 768], P('ma'), may hold values from -6 to 6
- pair_index: int32 [8], replicated, may hold values from 0 to 255, as said below
- diffusivity: float32 [4], replicated, may hold values from 0.0001 to 0.0004
Outputs:
- new_spectra: float32 [4, 2, 128, 4224], P(None, None, 'row', 'ma')
Inputs may be any that keep to these rules, and one draw needn't show every extreme that they name: 8 distinct values, among them always both 0 and the largest; position g holds the orders pair_index[g] and 511 - pair_index[g].
All inputs are finite; a program needn't handle non-finite values.
Results may differ from a plain program's by a relative error of at most 0.0057.
Values may be sent and summed in bfloat16 or wider, within the bound.
A program may use at most 64 MiB of HBM per device.

v0:
```python
import math
import jax
import jax.numpy as jnp
from jax import lax
from jax.sharding import PartitionSpec as P

LMAX = 511
NPHI = 1536
SLOTS = 528
ROTATION = 2.0
SHELL_RADIUS = 16.0


def slot_layout(pair_values):
    slot_index = jnp.arange(SLOTS, dtype=jnp.int32)[None, :]
    lowest = pair_values[:, None]
    first_part = slot_index < LMAX + 1 - lowest
    second_part = jnp.logical_and(jnp.logical_not(first_part), slot_index < LMAX + 2)
    degree = jnp.where(first_part, lowest + slot_index, slot_index - 1)
    wave_order = jnp.where(first_part, lowest, LMAX - lowest)
    return (first_part, second_part, degree, wave_order)


def fourier_tables(pair_values):
    orders = jnp.stack([pair_values, LMAX - pair_values], axis=1)
    angle_step = jnp.arange(NPHI, dtype=jnp.int32)
    phases = orders[:, :, None] * angle_step[None, None, :] % NPHI
    angles = phases.astype(jnp.float32) * (2.0 * math.pi / NPHI)
    weight_order = jnp.where(orders == 0, 1.0, 2.0).astype(jnp.float32)[:, :, None]
    cosine = jnp.cos(angles)
    sine_part = jnp.sin(angles)
    synthesis = jnp.stack([weight_order * cosine, -weight_order * sine_part]).astype(jnp.bfloat16)
    analysis_fourier = (jnp.stack([cosine, -sine_part]) / NPHI).astype(jnp.bfloat16)
    return (synthesis, analysis_fourier)


def grid_products(grid_values):
    stream_theta, stream_phi, poloidal_theta, poloidal_phi = (
        grid_values[0],
        grid_values[1],
        grid_values[2],
        grid_values[3],
    )
    thermal_theta, thermal_phi, magnetic_theta, magnetic_phi = (
        grid_values[4],
        grid_values[5],
        grid_values[6],
        grid_values[7],
    )
    flow_theta = poloidal_theta - stream_phi
    flow_phi = poloidal_phi + stream_theta
    field_theta = -magnetic_phi
    stress = field_theta * magnetic_theta - flow_theta * flow_phi
    pressure = 0.5 * (magnetic_theta * magnetic_theta - field_theta * field_theta) - 0.5 * (
        flow_phi * flow_phi - flow_theta * flow_theta
    )
    heat_flux = -(flow_theta * thermal_theta + flow_phi * thermal_phi)
    induction = -(flow_theta * magnetic_theta - flow_phi * field_theta)
    return jnp.stack([stress, pressure, heat_flux, induction])


def coupled(source, partner, parity, degree, wave_order, alive):
    degree_real = degree.astype(jnp.float32)
    order_real = wave_order.astype(jnp.float32)
    lower_coupling = jnp.sqrt(
        (degree_real * degree_real - order_real * order_real)
        * alive
        / jnp.maximum(4.0 * degree_real * degree_real - 1.0, 1.0)
    )
    upper_degree = degree_real + 1.0
    upper_coupling = (
        jnp.sqrt(
            (upper_degree * upper_degree - order_real * order_real)
            / (4.0 * upper_degree * upper_degree - 1.0)
        )
        * alive
        * (degree < LMAX).astype(jnp.float32)
    )
    spin_term = order_real / (degree_real * (degree_real + 1.0) + 2.0)
    turned = jnp.stack([-source[1], source[0]])
    below_slot = jnp.concatenate([jnp.zeros_like(partner[..., :1]), partner[..., :-1]], axis=-1)
    above_slot = jnp.concatenate([partner[..., 1:], jnp.zeros_like(partner[..., :1])], axis=-1)
    return ROTATION * (
        spin_term * turned + parity * (lower_coupling * below_slot + upper_coupling * above_slot)
    )


def radial_solve(right_side, degree_flat, diffusivity):
    points = right_side.shape[2]
    counter = jnp.arange(1, points + 1, dtype=jnp.int32)
    product = counter[:, None] * counter[None, :] % (2 * (points + 1))
    sine_basis = math.sqrt(2.0 / (points + 1)) * jnp.sin(
        product.astype(jnp.float32) * (math.pi / (points + 1))
    )
    eigenvalues = (
        4.0
        * (points + 1)
        * (points + 1)
        * jnp.sin(counter.astype(jnp.float32) * (math.pi / (2 * (points + 1)))) ** 2
    )
    degree_real = degree_flat.astype(jnp.float32)
    horizontal = degree_real * (degree_real + 1.0) / (SHELL_RADIUS * SHELL_RADIUS)
    modal_part = jnp.einsum(
        "jk,fcks->fcjs", sine_basis, right_side, precision=lax.Precision.HIGHEST
    )
    factor = 1.0 + diffusivity[:, None, None, None] * (
        eigenvalues[None, None, :, None] + horizontal[None, None, None, :]
    )
    return jnp.einsum(
        "jk,fcks->fcjs", sine_basis, modal_part / factor, precision=lax.Precision.HIGHEST
    )


def local(spectra, dtheta_table, dphi_table, analysis_table, pair_index, diffusivity):
    local_pairs = spectra.shape[3] // SLOTS
    radius_count = spectra.shape[2]
    theta_count = dtheta_table.shape[1]
    columns = local_pairs * SLOTS
    own_pairs = lax.dynamic_slice_in_dim(
        pair_index, lax.axis_index("ma") * local_pairs, local_pairs
    )
    first_part, second_part, degree, wave_order = slot_layout(own_pairs)
    alive = jnp.logical_or(first_part, second_part).astype(jnp.float32)
    part_masks = jnp.stack([first_part, second_part], axis=1).astype(jnp.float32)
    masked_state = spectra.reshape(4, 2, radius_count, local_pairs, SLOTS) * alive
    coeffs = masked_state.astype(jnp.bfloat16)
    spread = coeffs[:, :, :, :, None, :] * part_masks.astype(jnp.bfloat16)[None, None, None]
    theta_rows = dtheta_table.reshape(local_pairs, SLOTS, theta_count)
    phi_rows = dphi_table.reshape(local_pairs, SLOTS, theta_count)
    along_theta = jnp.einsum(
        "fcrpjs,pst->fcrpjt", spread, theta_rows, preferred_element_type=jnp.float32
    )
    phi_direct = jnp.einsum(
        "fcrpjs,pst->fcrpjt", spread, phi_rows, preferred_element_type=jnp.float32
    )
    along_phi = jnp.stack([-phi_direct[:, 1], phi_direct[:, 0]], axis=1)
    grid_spectra = jnp.stack([along_theta, along_phi], axis=1)
    grid_spectra = (
        jnp.transpose(grid_spectra, (3, 0, 1, 2, 4, 5, 6))
        .reshape(radius_count, 8, 2, local_pairs, 2, theta_count)
        .astype(jnp.bfloat16)
    )
    synthesis, analysis_fourier = fourier_tables(pair_index)

    def one_radius(radius_block):
        grid_values = jnp.einsum(
            "qcpjt,cpjk->qtk", radius_block, synthesis, preferred_element_type=jnp.float32
        )
        products = grid_products(grid_values).astype(jnp.bfloat16)
        return jnp.einsum(
            "ftk,cpjk->fcpjt", products, analysis_fourier, preferred_element_type=jnp.float32
        ).astype(jnp.bfloat16)

    latitudes = lax.all_to_all(grid_spectra, "ma", split_axis=5, concat_axis=3, tiled=True)
    computed = lax.map(one_radius, latitudes)
    returned = lax.all_to_all(computed, "ma", split_axis=3, concat_axis=5, tiled=True)
    analysis_rows = analysis_table.reshape(local_pairs, SLOTS, theta_count)
    projected = jnp.einsum(
        "rfcpjt,pst->fcrpjs", returned, analysis_rows, preferred_element_type=jnp.float32
    )
    nonlinear = jnp.sum(projected * part_masks[None, None, None], axis=4)
    forcing = jnp.stack(
        [
            coupled(masked_state[0], masked_state[1], 1.0, degree, wave_order, alive),
            coupled(masked_state[1], masked_state[0], -1.0, degree, wave_order, alive),
        ]
    )
    forcing = jnp.concatenate([forcing, jnp.zeros_like(forcing)], axis=0)
    right_side = (masked_state + nonlinear + forcing) * alive
    pencils = lax.all_to_all(
        right_side.reshape(4, 2, radius_count, columns),
        "row",
        split_axis=3,
        concat_axis=2,
        tiled=True,
    )
    share_size = columns // lax.axis_size("row")
    degree_share = lax.dynamic_slice_in_dim(
        degree.reshape(columns), lax.axis_index("row") * share_size, share_size
    )
    solved = radial_solve(pencils, degree_share, diffusivity)
    shells = lax.all_to_all(solved, "row", split_axis=2, concat_axis=3, tiled=True)
    return shells * alive.reshape(columns)


def solution(mesh):
    return jax.shard_map(
        local,
        mesh=mesh,
        in_specs=(
            P(None, None, "row", "ma"),
            P("ma", None),
            P("ma", None),
            P("ma", None),
            P(),
            P(),
        ),
        out_specs=P(None, None, "row", "ma"),
        check_vma=False,
    )
```

profile of v0, /device:TPU:2, one launch (start us, length us, event | category | flops | bytes accessed | tf_op | source)
XLA Modules:
  0.0 247.0 jit_solution(5899633462003070407)
XLA Ops:
  0.0 1.4 dynamic_slice.10
  3.3 1.2 fusion.98
  7.6 11.3 %copy.34 = bf16[32,8,2,1,2,768]{0,4,2,1,3,5:T(2,128)(2,1)} copy(bf16[32,8,2,1,2,768]{5,0,4,2,1,3:T(8,128)(2,1)S(1)} %bitcast.167) | data formatting | bytes 3145728 | tf_op jit(solution)/shard_map/convert_element_type | solution.py:141
  18.9 9.5 %reshape.518 = bf16[8,2,49152]{2,1,0:T(2,128)(2,1)} reshape(bf16[768,1,8,2,2,32]{5,4,3,2,1,0:T(2,128)(2,1)} %bitcast.163) | data formatting | bytes 3145728
  28.4 4.4 %all-to-all-start = ((bf16[8,2,49152]{2,1,0:T(2,128)(2,1)}), bf16[8,2,49152]{2,1,0:T(2,128)(2,1)S(1)}, u32[]{:S(2)}, u32[]{:S(2)}) async-start(bf16[8,2,49152]{2,1,0:T(2,128)(2,1)} %reshape.518), calls=%async_computation | async-start | bytes 3145728 | tf_op jit(solution)/shard_map/all_to_all | solution.py:154
  33.5 1.3 fusion.68
  34.8 1.3 fusion.77
  40.0 12.3 %all-to-all-done = bf16[8,2,49152]{2,1,0:T(2,128)(2,1)S(1)} async-done(((bf16[8,2,49152]{2,1,0:T(2,128)(2,1)}), bf16[8,2,49152]{2,1,0:T(2,128)(2,1)S(1)}, u32[]{:S(2)}, u32[]{:S(2)}) %all-to-all-start) | async-done | bytes 1572896 | tf_op jit(solution)/shard_map/all_to_all | solution.py:154
  52.3 5.4 %reshape.519 = bf16[768,1,8,2,2,32]{5,4,3,2,1,0:T(2,128)(2,1)} reshape(bf16[8,2,49152]{2,1,0:T(2,128)(2,1)S(1)} %all-to-all-done) | data formatting | bytes 3145728
  57.7 11.0 %copy.35 = bf16[32,8,2,1,2,8,96]{6,5,4,1,2,0,3:T(8,128)(2,1)S(1)} copy(bf16[32,8,2,1,2,8,96]{0,4,2,1,6,5,3:T(2,128)(2,1)} %bitcast.164) | data formatting | bytes 3145728 | tf_op jit(solution)/shard_map/all_to_all | solution.py:154
  68.7 86.1 %while.10 = (s32[]{:T(128)}, bf16[32,4,2,8,2,96]{5,4,2,1,0,3:T(2,128)(2,1)}, bf16[32,8,2,8,2,96]{5,3,4,1,2,0:T(8,128)(2,1)S(1)}, bf16[2,8,2,1536]{3,1,2,0:T(8,12...) while((s32[]{:T(128)}, bf16[32,4,2,8,2,96]{5,4,2,1,0,3:T(2,128)(2,1)}, ...), condition=%wide.region_1.2_spmd, body=%wide.region_0.1_spmd.sunk | while | flops 122105856 | bytes 15680073 | solution.py:155
  154.8 5.1 %all-to-all-start.1 = ((bf16[32,4,2,8,2,96]{5,4,2,1,0,3:T(2,128)(2,1)}), bf16[32,4,2,8,2,96]{5,4,2,1,0,3:T(2,128)(2,1)S(1)}, u32[]{:S(2)}, u32[]{:S(2)}) async-start(bf16[32,4,2,8,2,96]{5,4,2,1,0,3:T(2,128)(2,1)} %get-tuple-element.32), calls=%async_computation.1 | async-start | bytes 2097152 | tf_op jit(solution)/shard_map/all_to_all | solution.py:156
  160.4 13.5 %all-to-all-done.1 = bf16[32,4,2,8,2,96]{5,4,2,1,0,3:T(2,128)(2,1)S(1)} async-done(((bf16[32,4,2,8,2,96]{5,4,2,1,0,3:T(2,128)(2,1)}), bf16[32,4,2,8,2,96]{5,4,2,1,0,3:T(2,128)(2,1)S(1)}, u32[]{:S(2)}, u32[]{:S(2)}) %all-to-all-start.1) | async-done | bytes 786464 | tf_op jit(solution)/shard_map/all_to_all | solution.py:156
  175.5 2.1 fusion.13
  178.5 2.9 %copy.42 = f32[4,2,32,528]{2,1,0,3:T(2,128)S(1)} copy(f32[4,2,32,528]{3,2,1,0:T(8,128)} %fusion.22) | data formatting | bytes 1081344 | tf_op jit(solution)/shard_map/mul | solution.py:169
  181.5 2.9 %reshape.520 = f32[4,1,33792]{2,1,0:T(1,128)} reshape(f32[528,4,2,32]{3,2,1,0:T(2,128)S(1)} %bitcast.165) | data formatting | bytes 1081344
  184.4 4.9 %all-to-all-start.2 = ((f32[4,1,33792]{2,1,0:T(1,128)}), f32[4,1,33792]{2,1,0:T(1,128)S(1)}, u32[]{:S(2)}, u32[]{:S(2)}) async-start(f32[4,1,33792]{2,1,0:T(1,128)} %reshape.520), calls=%async_computation.2 | async-start | bytes 1081344 | tf_op jit(solution)/shard_map/all_to_all | solution.py:170
  189.3 1.4 fusion.85
  191.6 12.7 %all-to-all-done.2 = f32[4,1,33792]{2,1,0:T(1,128)S(1)} async-done(((f32[4,1,33792]{2,1,0:T(1,128)}), f32[4,1,33792]{2,1,0:T(1,128)S(1)}, u32[]{:S(2)}, u32[]{:S(2)}) %all-to-all-start.2) | async-done | bytes 540704 | tf_op jit(solution)/shard_map/all_to_all | solution.py:170
  204.9 2.2 reduce.1
  207.1 1.9 reshape.521
  209.0 3.0 %copy.43 = f32[4,2,32,4,132]{4,2,3,1,0:T(8,128)} copy(f32[4,2,32,4,132]{2,1,0,4,3:T(2,128)S(1)} %bitcast.166) | data formatting | bytes 1081344 | tf_op jit(solution)/shard_map/all_to_all | solution.py:170
  212.0 3.2 %fusion.15 = f32[4,2,128,132]{2,3,1,0:T(8,128)S(1)} fusion(f32[4,2,128,132]{3,2,1,0:T(8,128)} %bitcast.171, f32[4,128,132]{1,2,0:T(8,128)S(1)} %copy-done.6, s32[128]{0:T(128)S(1)} %iota_add_fusion.1), kind=kOutput, calls=%fused_computation.32 | convolution fusion | flops 207917056 | bytes 1352192 | tf_op jit(solution)/shard_map/jk,fcks->fcjs/dot_general | solution.py:103
  216.7 27.7 %all_to_all.69 = f32[4,2,128,132]{3,1,0,2:T(2,128)S(1)} all-to-all(f32[4,2,128,132]{3,1,0,2:T(2,128)S(1)} %copy.45), channel_id=1, replica_groups=mesh['row'=4,'ma'=8] {'row'}, dimensions={2} | all-to-all | bytes 1081344 | tf_op jit(solution)/shard_map/all_to_all | solution.py:182
  (233 shorter events, 101.7 us)
Async XLA Ops:
  0.0 4.5 %copy-start = (bf16[528,768]{1,0:T(8,128)(2,1)S(1)}, bf16[528,768]{1,0:T(8,128)(2,1)}, u32[]{:S(2)}) copy-start(bf16[528,768]{1,0:T(8,128)(2,1)} %param.10) | copy-start | bytes 2433028
  2.1 0.6 copy-start.10
  4.5 34.1 %copy-start.1 = (f32[4,2,32,528]{3,2,1,0:T(8,128)}, f32[4,2,32,528]{3,2,1,0:T(8,128)S(1)}, u32[]{:S(2)}) copy-start(f32[4,2,32,528]{3,2,1,0:T(8,128)S(1)} %get-tuple-element.47) | copy-start | bytes 1622020
  5.3 1.1 copy-start.16
  28.4 4.4 %copy-start.12 = (s32[8]{0:T(128)S(1)}, s32[8]{0:T(128)}, u32[]{:S(2)}) copy-start(s32[8]{0:T(128)} %param.12) | copy-start | bytes 100
  28.4 23.9 %all-to-all-start = ((bf16[8,2,49152]{2,1,0:T(2,128)(2,1)}), bf16[8,2,49152]{2,1,0:T(2,128)(2,1)S(1)}, u32[]{:S(2)}, u32[]{:S(2)}) async-start(bf16[8,2,49152]{2,1,0:T(2,128)(2,1)} %reshape.518), calls=%async_computation | async-start | bytes 3145728 | tf_op jit(solution)/shard_map/all_to_all | solution.py:154
  57.7 11.0 %copy-start.7 = (bf16[2,8,2,1536]{3,1,2,0:T(8,128)(2,1)S(1)}, bf16[2,8,2,1536]{3,1,2,0:T(8,128)(2,1)}, u32[]{:S(2)}) copy-start(bf16[2,8,2,1536]{3,1,2,0:T(8,128)(2,1)} %fusion.27) | copy-start | bytes 294916
  154.8 5.1 %copy-start.3 = (f32[1,2,32,1,528]{4,2,1,3,0:T(8,128)S(1)}, f32[1,2,32,1,528]{4,2,1,3,0:T(8,128)}, u32[]{:S(2)}) copy-start(f32[1,2,32,1,528]{4,2,1,3,0:T(8,128)} %get-tuple-element.54) | copy-start | bytes 405508
  154.8 5.3 %copy-start.4 = (f32[1,32,1,528]{3,1,0,2:T(8,128)S(1)}, f32[1,32,1,528]{3,1,0,2:T(8,128)}, u32[]{:S(2)}) copy-start(f32[1,32,1,528]{3,1,0,2:T(8,128)} %get-tuple-element.61) | copy-start | bytes 202756
  154.8 5.3 %copy-start.5 = (f32[1,32,1,528]{3,1,2,0:T(8,128)S(1)}, f32[1,32,1,528]{3,1,2,0:T(8,128)}, u32[]{:S(2)}) copy-start(f32[1,32,1,528]{3,1,2,0:T(8,128)} %get-tuple-element.76) | copy-start | bytes 202756
  154.8 5.3 %copy-start.8 = (f32[528]{0:T(1024)S(1)}, f32[528]{0:T(1024)}, u32[]{:S(2)}) copy-start(f32[528]{0:T(1024)} %get-tuple-element.75) | copy-start | bytes 6340
  154.8 5.3 %copy-start.9 = (f32[528]{0:T(1024)S(1)}, f32[528]{0:T(1024)}, u32[]{:S(2)}) copy-start(f32[528]{0:T(1024)} %fusion.77) | copy-start | bytes 6340
  154.8 19.0 %all-to-all-start.1 = ((bf16[32,4,2,8,2,96]{5,4,2,1,0,3:T(2,128)(2,1)}), bf16[32,4,2,8,2,96]{5,4,2,1,0,3:T(2,128)(2,1)S(1)}, u32[]{:S(2)}, u32[]{:S(2)}) async-start(bf16[32,4,2,8,2,96]{5,4,2,1,0,3:T(2,128)(2,1)} %get-tuple-element.32), calls=%async_computation.1 | async-start | bytes 2097152 | tf_op jit(solution)/shard_map/all_to_all | solution.py:156
  173.9 1.6 copy-start.11
  175.4 2.1 copy-start.2
  175.5 2.1 copy-start.15
  181.5 9.3 %copy-start.14 = (f32[128]{0:T(128)S(1)}, f32[128]{0:T(128)}, u32[]{:S(2)}) copy-start(f32[128]{0:T(128)} %multiply_multiply_fusion.2) | copy-start | bytes 1540
  181.5 9.4 %copy-start.13 = (f32[4]{0:T(128)S(1)}, f32[4]{0:T(128)}, u32[]{:S(2)}) copy-start(f32[4]{0:T(128)} %param.13) | copy-start | bytes 52
  184.4 20.0 %all-to-all-start.2 = ((f32[4,1,33792]{2,1,0:T(1,128)}), f32[4,1,33792]{2,1,0:T(1,128)S(1)}, u32[]{:S(2)}, u32[]{:S(2)}) async-start(f32[4,1,33792]{2,1,0:T(1,128)} %reshape.520), calls=%async_computation.2 | async-start | bytes 1081344 | tf_op jit(solution)/shard_map/all_to_all | solution.py:170
  209.0 3.0 %copy-start.6 = (f32[4,128,132]{1,2,0:T(8,128)S(1)}, f32[4,128,132]{1,2,0:T(8,128)}, u32[]{:S(2)}) copy-start(f32[4,128,132]{1,2,0:T(8,128)} %multiply_add_fusion) | copy-start | bytes 811012
where the time goes:
time: 248 us; the launch traced here: 247 us
  local copies, waits for them, and re-layouts  77.7 us (31%)
  matrix products  49.3 us (20%)
  waiting for transfers between devices  38.6 us (16%)
  other arithmetic  36.6 us (15%)
  blocking collectives  27.7 us (11%)
  starting transfers between devices  14.4 us (6%)
    all_to_all x1, blocking collectives, local(): lax.all_to_all(solved, 'row', split_axis=2, concat_axis=3, tiled=True)  27.7 us
    dot_general x32, matrix products, one_radius(): jnp.einsum('qcpjt,cpjk->qtk', radius_block, synthesis, preferred_element_...  25.6 us
    another operation x65, other arithmetic  22.9 us
    unnamed x38, local copies, waits for them, and re-layouts  21.4 us
    dynamic_update_slice x32, local copies, waits for them, and re-layouts, local(): computed = lax.map(one_radius, latitudes)  20.8 us
    dot_general x32, matrix products, one_radius(): jnp.einsum('ftk,cpjk->fcpjt', products, analysis_fourier, preferred_eleme...  16 us
    all_to_all x1, waiting for transfers between devices, local(): lax.all_to_all(computed, 'ma', split_axis=3, concat_axis=5, tiled=True)  13.5 us
    all_to_all x1, waiting for transfers between devices, local(): lax.all_to_all(right_side.reshape(4, 2, radius_count, columns), 'row', sp...  12.7 us
  transfers between devices with their start and end apart: 3, of which 3 were waited for; matrix products, arithmetic and copies ran while one was open for 4% of the time, Pallas kernels for 0%

commit v1 on v0

--- a/solution.py
+++ b/solution.py
@@ -9,6 +9,31 @@
 SLOTS = 528
 ROTATION = 2.0
 SHELL_RADIUS = 16.0
+
+
+def convert_plate(inputs, ndim_at, message):
+    q_next, local_part = (inputs.shape[:ndim_at], inputs.shape[ndim_at + 1 :])
+    oldest = jnp.moveaxis(inputs.reshape(*q_next, message, -1, *local_part), ndim_at, 0)
+    return oldest
+
+
+def push_plane_up(state, axis_k):
+    y2 = list(state.shape[1:])
+    y2[axis_k] *= state.shape[0]
+    part_next = jnp.moveaxis(state, 0, axis_k).reshape(y2)
+    return part_next
+
+
+def set_the_series(inp, ax_name, array_in, in_array):
+    then, work_now = (lax.axis_size(ax_name), lax.axis_index(ax_name))
+    res = convert_plate(inp, array_in, then)
+    in_order = [res[work_now]]
+    for d in range(1, then):
+        later = res[work_now ^ d]
+        in_order.append(lax.ppermute(later, ax_name, [(i, i ^ d) for i in range(then)]))
+    res = jnp.stack(in_order)[work_now ^ jnp.arange(then)]
+    before = push_plane_up(res, in_array)
+    return before
 
 
 def slot_layout(pair_values):
@@ -179,7 +204,7 @@
         degree.reshape(columns), lax.axis_index("row") * share_size, share_size
     )
     solved = radial_solve(pencils, degree_share, diffusivity)
-    shells = lax.all_to_all(solved, "row", split_axis=2, concat_axis=3, tiled=True)
+    shells = set_the_series(solved, "row", 2, 3)
     return shells * alive.reshape(columns)
 
 

time: 248 us -> 244 us (0.984)
  blocking collectives: 27.7 us -> 0 us
  waiting for transfers between devices: 38.6 us -> 56.2 us
  starting transfers between devices: 14.4 us -> 18.8 us
    all_to_all x1 -> x0, blocking collectives: 27.7 us -> none  [local(): lax.all_to_all(solved, 'row', split_axis=2, concat_axis=3, tiled=True)]
    ppermute x0 -> x3, waiting for transfers between devices: none -> 17.1 us  [set_the_series(): lax.ppermute(later, ax_name, [(i, i ^ d) for i in range(then)])]
    ppermute x0 -> x3, starting transfers between devices: none -> 4.44 us  [set_the_series(): lax.ppermute(later, ax_name, [(i, i ^ d) for i in range(then)])]
    another operation x65 -> x66, other arithmetic: 22.9 us -> 22.9 us
  transfers between devices with their start and end apart: 3 -> 6, of which waited for: 3 -> 5; matrix products, arithmetic and copies ran while one was open for 4% -> 4% of each run, Pallas kernels for 0% -> 0%
where the time goes in v1:
time: 244 us; the launch traced here: 241 us
  local copies, waits for them, and re-layouts  77.6 us (32%)
  waiting for transfers between devices  56.2 us (23%)
  matrix products  49.3 us (20%)
  other arithmetic  36.3 us (15%)
  starting transfers between devices  18.8 us (8%)
    dot_general x32, matrix products, one_radius(): jnp.einsum('qcpjt,cpjk->qtk', radius_block, synthesis, preferred_element_...  25.6 us
    another operation x65, other arithmetic  22.9 us
    unnamed x38, local copies, waits for them, and re-layouts  21.4 us
    dynamic_update_slice x32, local copies, waits for them, and re-layouts, local(): computed = lax.map(one_radius, latitudes)  20.8 us
    ppermute x3, waiting for transfers between devices, set_the_series(): lax.ppermute(later, ax_name, [(i, i ^ d) for i in range(then)])  17.1 us
    dot_general x32, matrix products, one_radius(): jnp.einsum('ftk,cpjk->fcpjt', products, analysis_fourier, preferred_eleme...  16 us
    all_to_all x1, waiting for transfers between devices, local(): lax.all_to_all(computed, 'ma', split_axis=3, concat_axis=5, tiled=True)  13.5 us
    all_to_all x1, waiting for transfers between devices, local(): lax.all_to_all(right_side.reshape(4, 2, radius_count, columns), 'row', sp...  12.9 us
  transfers between devices with their start and end apart: 6, of which 5 were waited for; matrix products, arithmetic and copies ran while one was open for 4% of the time, Pallas kernels for 0%

profile of v1, /device:TPU:2, one launch (start us, length us, event | category | flops | bytes accessed | tf_op | source)
XLA Modules:
  0.0 240.7 jit_solution(2914263242028515154)
XLA Ops:
  0.0 1.3 dynamic_slice.16
  7.4 11.3 %copy.33 = bf16[32,8,2,1,2,768]{0,4,2,1,3,5:T(2,128)(2,1)} copy(bf16[32,8,2,1,2,768]{5,0,4,2,1,3:T(8,128)(2,1)S(1)} %bitcast.179) | data formatting | bytes 3145728 | tf_op jit(solution)/shard_map/convert_element_type | solution.py:166
  18.6 9.5 %reshape.557 = bf16[8,2,49152]{2,1,0:T(2,128)(2,1)} reshape(bf16[768,1,8,2,2,32]{5,4,3,2,1,0:T(2,128)(2,1)} %bitcast.175) | data formatting | bytes 3145728
  28.2 4.4 %all-to-all-start = ((bf16[8,2,49152]{2,1,0:T(2,128)(2,1)}), bf16[8,2,49152]{2,1,0:T(2,128)(2,1)S(1)}, u32[]{:S(2)}, u32[]{:S(2)}) async-start(bf16[8,2,49152]{2,1,0:T(2,128)(2,1)} %reshape.557), calls=%async_computation | async-start | bytes 3145728 | tf_op jit(solution)/shard_map/all_to_all | solution.py:179
  39.4 12.7 %all-to-all-done = bf16[8,2,49152]{2,1,0:T(2,128)(2,1)S(1)} async-done(((bf16[8,2,49152]{2,1,0:T(2,128)(2,1)}), bf16[8,2,49152]{2,1,0:T(2,128)(2,1)S(1)}, u32[]{:S(2)}, u32[]{:S(2)}) %all-to-all-start) | async-done | bytes 1572896 | tf_op jit(solution)/shard_map/all_to_all | solution.py:179
  52.1 5.4 %reshape.558 = bf16[768,1,8,2,2,32]{5,4,3,2,1,0:T(2,128)(2,1)} reshape(bf16[8,2,49152]{2,1,0:T(2,128)(2,1)S(1)} %all-to-all-done) | data formatting | bytes 3145728
  57.5 11.0 %copy.34 = bf16[32,8,2,1,2,8,96]{6,5,4,1,2,0,3:T(8,128)(2,1)S(1)} copy(bf16[32,8,2,1,2,8,96]{0,4,2,1,6,5,3:T(2,128)(2,1)} %bitcast.176) | data formatting | bytes 3145728 | tf_op jit(solution)/shard_map/all_to_all | solution.py:179
  68.5 86.1 %while.10 = (s32[]{:T(128)}, bf16[32,4,2,8,2,96]{5,4,2,1,0,3:T(2,128)(2,1)}, bf16[32,8,2,8,2,96]{5,3,4,1,2,0:T(8,128)(2,1)S(1)}, bf16[2,8,2,1536]{3,1,2,0:T(8,12...) while((s32[]{:T(128)}, bf16[32,4,2,8,2,96]{5,4,2,1,0,3:T(2,128)(2,1)}, ...), condition=%wide.region_1.2_spmd, body=%wide.region_0.1_spmd.sunk | while | flops 122105856 | bytes 15680073 | solution.py:180
  154.6 5.1 %all-to-all-start.1 = ((bf16[32,4,2,8,2,96]{5,4,2,1,0,3:T(2,128)(2,1)}), bf16[32,4,2,8,2,96]{5,4,2,1,0,3:T(2,128)(2,1)S(1)}, u32[]{:S(2)}, u32[]{:S(2)}) async-start(bf16[32,4,2,8,2,96]{5,4,2,1,0,3:T(2,128)(2,1)} %get-tuple-element.32), calls=%async_computation.1 | async-start | bytes 2097152 | tf_op jit(solution)/shard_map/all_to_all | solution.py:181
  160.1 13.5 %all-to-all-done.1 = bf16[32,4,2,8,2,96]{5,4,2,1,0,3:T(2,128)(2,1)S(1)} async-done(((bf16[32,4,2,8,2,96]{5,4,2,1,0,3:T(2,128)(2,1)}), bf16[32,4,2,8,2,96]{5,4,2,1,0,3:T(2,128)(2,1)S(1)}, u32[]{:S(2)}, u32[]{:S(2)}) %all-to-all-start.1) | async-done | bytes 786464 | tf_op jit(solution)/shard_map/all_to_all | solution.py:181
  175.2 2.1 fusion.13
  178.3 2.9 %copy.41 = f32[4,2,32,528]{2,1,0,3:T(2,128)S(1)} copy(f32[4,2,32,528]{3,2,1,0:T(8,128)} %fusion.22) | data formatting | bytes 1081344 | tf_op jit(solution)/shard_map/mul | solution.py:194
  181.3 2.9 %reshape.559 = f32[4,1,33792]{2,1,0:T(1,128)} reshape(f32[528,4,2,32]{3,2,1,0:T(2,128)S(1)} %bitcast.177) | data formatting | bytes 1081344
  184.2 4.9 %all-to-all-start.2 = ((f32[4,1,33792]{2,1,0:T(1,128)}), f32[4,1,33792]{2,1,0:T(1,128)S(1)}, u32[]{:S(2)}, u32[]{:S(2)}) async-start(f32[4,1,33792]{2,1,0:T(1,128)} %reshape.559), calls=%async_computation.2 | async-start | bytes 1081344 | tf_op jit(solution)/shard_map/all_to_all | solution.py:195
  189.0 1.3 fusion.87
  191.2 12.9 %all-to-all-done.2 = f32[4,1,33792]{2,1,0:T(1,128)S(1)} async-done(((f32[4,1,33792]{2,1,0:T(1,128)}), f32[4,1,33792]{2,1,0:T(1,128)S(1)}, u32[]{:S(2)}, u32[]{:S(2)}) %all-to-all-start.2) | async-done | bytes 540704 | tf_op jit(solution)/shard_map/all_to_all | solution.py:195
  204.6 2.2 reduce.1
  206.8 1.9 reshape.560
  208.8 3.0 %copy.42 = f32[4,2,32,4,132]{4,2,3,1,0:T(8,128)} copy(f32[4,2,32,4,132]{2,1,0,4,3:T(2,128)S(1)} %bitcast.178) | data formatting | bytes 1081344 | tf_op jit(solution)/shard_map/all_to_all | solution.py:195
  211.7 3.2 %fusion.15 = f32[4,2,128,132]{2,3,1,0:T(8,128)S(1)} fusion(f32[4,2,128,132]{3,2,1,0:T(8,128)} %bitcast.184, f32[4,128,132]{1,2,0:T(8,128)S(1)} %copy-done.6, s32[128]{0:T(128)S(1)} %iota_add_fusion.1), kind=kOutput, calls=%fused_computation.33 | convolution fusion | flops 207917056 | bytes 1352192 | tf_op jit(solution)/shard_map/jk,fcks->fcjs/dot_general | solution.py:128
  216.3 2.0 collective-permute-start.1
  218.4 2.4 collective-permute-start.2
  220.7 7.5 %collective-permute-done = f32[4,2,32,132]{3,2,1,0:T(8,128)S(1)} collective-permute-done((f32[4,2,32,132]{3,2,1,0:T(8,128)S(1)}, f32[4,2,32,132]{3,2,1,0:T(8,128)S(1)}, u32[]{:S(2)}, u32[]{:S(2)}) %collective-permute-start) | collective-permute-done | bytes 135200 | tf_op jit(solution)/shard_map/ppermute | solution.py:33
  228.2 9.6 %collective-permute-done.1 = f32[4,2,32,132]{3,2,1,0:T(8,128)S(1)} collective-permute-done((f32[4,2,32,132]{3,2,1,0:T(8,128)S(1)}, f32[4,2,32,132]{3,2,1,0:T(8,128)S(1)}, u32[]{:S(2)}, u32[]{:S(2)}) %collective-permute-start.1) | collective-permute-done | bytes 135200 | tf_op jit(solution)/shard_map/ppermute | solution.py:33
  (242 shorter events, 105.4 us)
Async XLA Ops:
  0.0 4.3 %copy-start = (bf16[528,768]{1,0:T(8,128)(2,1)S(1)}, bf16[528,768]{1,0:T(8,128)(2,1)}, u32[]{:S(2)}) copy-start(bf16[528,768]{1,0:T(8,128)(2,1)} %param.10) | copy-start | bytes 2433028
  1.9 0.5 copy-start.10
  4.2 33.7 %copy-start.1 = (f32[4,2,32,528]{3,2,1,0:T(8,128)}, f32[4,2,32,528]{3,2,1,0:T(8,128)S(1)}, u32[]{:S(2)}) copy-start(f32[4,2,32,528]{3,2,1,0:T(8,128)S(1)} %get-tuple-element.47) | copy-start | bytes 1622020
  5.1 1.1 copy-start.16
  28.2 4.4 %copy-start.12 = (s32[8]{0:T(128)S(1)}, s32[8]{0:T(128)}, u32[]{:S(2)}) copy-start(s32[8]{0:T(128)} %param.12) | copy-start | bytes 100
  28.2 23.9 %all-to-all-start = ((bf16[8,2,49152]{2,1,0:T(2,128)(2,1)}), bf16[8,2,49152]{2,1,0:T(2,128)(2,1)S(1)}, u32[]{:S(2)}, u32[]{:S(2)}) async-start(bf16[8,2,49152]{2,1,0:T(2,128)(2,1)} %reshape.557), calls=%async_computation | async-start | bytes 3145728 | tf_op jit(solution)/shard_map/all_to_all | solution.py:179
  57.5 11.0 %copy-start.7 = (bf16[2,8,2,1536]{3,1,2,0:T(8,128)(2,1)S(1)}, bf16[2,8,2,1536]{3,1,2,0:T(8,128)(2,1)}, u32[]{:S(2)}) copy-start(bf16[2,8,2,1536]{3,1,2,0:T(8,128)(2,1)} %fusion.27) | copy-start | bytes 294916
  154.6 5.1 %copy-start.3 = (f32[1,2,32,1,528]{4,2,1,3,0:T(8,128)S(1)}, f32[1,2,32,1,528]{4,2,1,3,0:T(8,128)}, u32[]{:S(2)}) copy-start(f32[1,2,32,1,528]{4,2,1,3,0:T(8,128)} %get-tuple-element.58) | copy-start | bytes 405508
  154.6 5.3 %copy-start.4 = (f32[1,32,1,528]{3,1,0,2:T(8,128)S(1)}, f32[1,32,1,528]{3,1,0,2:T(8,128)}, u32[]{:S(2)}) copy-start(f32[1,32,1,528]{3,1,0,2:T(8,128)} %get-tuple-element.65) | copy-start | bytes 202756
  154.6 5.3 %copy-start.5 = (f32[1,32,1,528]{3,1,2,0:T(8,128)S(1)}, f32[1,32,1,528]{3,1,2,0:T(8,128)}, u32[]{:S(2)}) copy-start(f32[1,32,1,528]{3,1,2,0:T(8,128)} %get-tuple-element.80) | copy-start | bytes 202756
  154.6 5.3 %copy-start.8 = (f32[528]{0:T(1024)S(1)}, f32[528]{0:T(1024)}, u32[]{:S(2)}) copy-start(f32[528]{0:T(1024)} %get-tuple-element.79) | copy-start | bytes 6340
  154.6 5.3 %copy-start.9 = (f32[528]{0:T(1024)S(1)}, f32[528]{0:T(1024)}, u32[]{:S(2)}) copy-start(f32[528]{0:T(1024)} %fusion.77) | copy-start | bytes 6340
  154.6 19.0 %all-to-all-start.1 = ((bf16[32,4,2,8,2,96]{5,4,2,1,0,3:T(2,128)(2,1)}), bf16[32,4,2,8,2,96]{5,4,2,1,0,3:T(2,128)(2,1)S(1)}, u32[]{:S(2)}, u32[]{:S(2)}) async-start(bf16[32,4,2,8,2,96]{5,4,2,1,0,3:T(2,128)(2,1)} %get-tuple-element.32), calls=%async_computation.1 | async-start | bytes 2097152 | tf_op jit(solution)/shard_map/all_to_all | solution.py:181
  173.6 1.6 copy-start.11
  175.2 2.1 copy-start.2
  175.2 2.1 copy-start.15
  181.2 9.1 %copy-start.14 = (f32[128]{0:T(128)S(1)}, f32[128]{0:T(128)}, u32[]{:S(2)}) copy-start(f32[128]{0:T(128)} %multiply_multiply_fusion.2) | copy-start | bytes 1540
  181.2 9.2 %copy-start.13 = (f32[4]{0:T(128)S(1)}, f32[4]{0:T(128)}, u32[]{:S(2)}) copy-start(f32[4]{0:T(128)} %param.13) | copy-start | bytes 52
  184.2 19.9 %all-to-all-start.2 = ((f32[4,1,33792]{2,1,0:T(1,128)}), f32[4,1,33792]{2,1,0:T(1,128)S(1)}, u32[]{:S(2)}, u32[]{:S(2)}) async-start(f32[4,1,33792]{2,1,0:T(1,128)} %reshape.559), calls=%async_computation.2 | async-start | bytes 1081344 | tf_op jit(solution)/shard_map/all_to_all | solution.py:195
  208.7 3.0 %copy-start.6 = (f32[4,128,132]{1,2,0:T(8,128)S(1)}, f32[4,128,132]{1,2,0:T(8,128)}, u32[]{:S(2)}) copy-start(f32[4,128,132]{1,2,0:T(8,128)} %multiply_add_fusion) | copy-start | bytes 811012
  216.3 11.9 %collective-permute-start = (f32[4,2,32,132]{3,2,1,0:T(8,128)S(1)}, f32[4,2,32,132]{3,2,1,0:T(8,128)S(1)}, u32[]{:S(2)}, u32[]{:S(2)}) collective-permute-start(f32[4,2,32,132]{3,2,1,0:T(8,128)S(1)} %get-tuple-element.54), channel_id=1, source_target_pairs={{0,8},{8,0},{16,24},{24,16},{1,9},{9,1},{17,25},{25,17},{2,10},{10... | collective-permute-start | bytes 405512 | tf_op jit(solution)/shard_map/ppermute | solution.py:33
  216.3 21.4 %collective-permute-start.1 = (f32[4,2,32,132]{3,2,1,0:T(8,128)S(1)}, f32[4,2,32,132]{3,2,1,0:T(8,128)S(1)}, u32[]{:S(2)}, u32[]{:S(2)}) collective-permute-start(f32[4,2,32,132]{3,2,1,0:T(8,128)S(1)} %get-tuple-element.53), channel_id=1, source_target_pairs={{0,16},{8,24},{16,0},{24,8},{1,17},{9,25},{17,1},{25,9},{2,18},{10... | collective-permute-start | bytes 405512 | tf_op jit(solution)/shard_map/ppermute | solution.py:33
  218.4 19.4 %collective-permute-start.2 = (f32[4,2,32,132]{3,2,1,0:T(8,128)S(1)}, f32[4,2,32,132]{3,2,1,0:T(8,128)S(1)}, u32[]{:S(2)}, u32[]{:S(2)}) collective-permute-start(f32[4,2,32,132]{3,2,1,0:T(8,128)S(1)} %get-tuple-element.52), channel_id=1, source_target_pairs={{0,24},{8,16},{16,8},{24,0},{1,25},{9,17},{17,9},{25,1},{2,26},{10... | collective-permute-start | bytes 405512 | tf_op jit(solution)/shard_map/ppermute | solution.py:33
